TPU v7x, 32 devices: a whole 2x2x4 slice. The times are simulated.
32 devices in a mesh: wide: 8 (over z, y), narrow: 4 (over x, core).
Axes of the slice: x: 2, y: 2, z: 4, core: 2. Of those that a mesh axis runs over, the one named last changes fastest.
Arguments:
- matrix_panel: float32 [8, 4194304], P(None, ('wide', 'narrow')), may hold values from -6 to 6
- sign_bits: int32 [4194304], P(('wide', 'narrow')), may hold values from 0 to 1
Outputs:
- mixed_panel: float32 [8, 4194304], P(None, ('wide', 'narrow'))
All inputs are finite; a program needn't handle non-finite values.
Results may differ from a plain program's by a relative error of at most 0.000086.
Values sent between devices are 32-bit elements; how exact they have to be, the bound alone decides.
A program may use at most 64 MiB of HBM per device.

v0:
```python
import math

import jax
import jax.numpy as jnp
from jax import lax
from jax.sharding import PartitionSpec as P


def swapped(shard, axis, distance):
    return lax.ppermute(shard, axis, [(i, i ^ 1 << distance) for i in range(lax.axis_size(axis))])


def hadamard_table(order):
    index = jnp.arange(order, dtype=jnp.int32)
    common = jnp.bitwise_and(index[:, None], index[None, :])
    parity = jnp.zeros((order, order), jnp.int32)
    for level in range(max(order.bit_length() - 1, 0)):
        parity = parity + jnp.bitwise_and(jnp.right_shift(common, level), 1)
    return (1 - 2 * jnp.bitwise_and(parity, 1)).astype(jnp.float32)


def local_transform(values):
    columns, length = values.shape
    factors = []
    remain = length
    while remain > 1:
        factor = min(128, remain)
        factors.insert(0, factor)
        remain = remain // factor
    before = 1
    for factor in factors:
        after = length // (before * factor)
        table = hadamard_table(factor)
        if after > 1:
            shaped = values.reshape(columns, before, factor, after)
            shaped = jnp.einsum("cafb,gf->cagb", shaped, table, precision=lax.Precision.HIGHEST)
        else:
            shaped = values.reshape(columns, before, factor)
            shaped = jnp.einsum("caf,gf->cag", shaped, table, precision=lax.Precision.HIGHEST)
        values = shaped.reshape(columns, length)
        before = before * factor
    return values


def body(matrix_panel, sign_bits):
    signed = matrix_panel * (2 * sign_bits - 1).astype(jnp.float32)[None, :]
    current = local_transform(signed)
    columns, length = current.shape
    wide_count = lax.axis_size("wide")
    narrow_count = lax.axis_size("narrow")
    position = lax.axis_index("narrow")
    for level in range(narrow_count.bit_length() - 1):
        partner = swapped(current, "narrow", level)
        upper_half = jnp.bitwise_and(jnp.right_shift(position, level), 1) == 1
        current = jnp.where(upper_half, partner - current, current + partner)
    wide_table = hadamard_table(wide_count)
    blocks = current.reshape(columns, wide_count, length // wide_count)
    mixed = jnp.einsum(
        "cwr,vw->cvr",
        lax.all_to_all(blocks, "wide", split_axis=1, concat_axis=1, tiled=True),
        wide_table,
        precision=lax.Precision.HIGHEST,
    )
    current = lax.all_to_all(mixed, "wide", split_axis=1, concat_axis=1, tiled=True).reshape(
        columns, length
    )
    scale = jnp.float32(1.0 / math.sqrt(length * wide_count * narrow_count))
    return current * scale


def solution(mesh):
    in_specs = (P(None, ("wide", "narrow")), P(("wide", "narrow")))
    out_specs = P(None, ("wide", "narrow"))
    return jax.shard_map(body, mesh=mesh, in_specs=in_specs, out_specs=out_specs, check_vma=False)
```

profile of v0, /device:TPU:11, one launch (start us, length us, event | category | flops | bytes accessed | tf_op | source)
XLA Modules:
  0.0 337.7 jit_solution(9903776614111497413)
XLA Ops:
  0.0 1.1 add_convert_fusion
  1.1 2.7 broadcast_multiply_fusion.1
  3.8 6.3 %fusion.5 = f32[8,8,128,128]{3,1,2,0:T(8,128)S(1)} fusion(f32[8,8,16384]{2,0,1:T(8,128)S(1)} %bitcast.36), kind=kOutput, calls=%fused_computation.9 | convolution fusion | flops 100664128 | bytes 8388608 | tf_op jit(solution)/shard_map/cafb,gf->cagb/dot_general | solution.py:36
  10.1 4.1 %fusion.1 = f32[128,8,8,128]{3,0,2,1:T(8,128)S(1)} fusion(f32[8,8,128,128]{3,1,2,0:T(8,128)S(1)} %fusion.5), kind=kOutput, calls=%fused_computation.3 | convolution fusion | flops 1611022336 | bytes 8388608 | tf_op jit(solution)/shard_map/cafb,gf->cagb/dot_general | solution.py:36
  14.2 3.7 %convolution_bitcast_fusion.1 = f32[1,8,1024,128]{3,2,1,0:T(8,128)S(1)} fusion(f32[8,1024,128]{2,1,0:T(8,128)S(1)} %bitcast.37), kind=kOutput, calls=%fused_computation.10 | convolution fusion | flops 1611022336 | bytes 8388608 | tf_op jit(solution)/shard_map/caf,gf->cag/dot_general | solution.py:39
  17.9 0.0 copy-start
  17.9 4.4 %copy.22 = f32[1,8,1024,128]{3,1,2,0:T(8,128)} copy(f32[1,8,1024,128]{3,2,1,0:T(8,128)S(1)} %convolution_bitcast_fusion.1) | data formatting | bytes 8388608
  22.3 0.0 copy-done
  22.3 0.7 collective-permute-start
  23.0 7.1 %collective-permute-done = f32[8,131072]{1,0:T(8,128)} collective-permute-done((f32[8,131072]{1,0:T(8,128)}, f32[8,131072]{1,0:T(8,128)}, u32[]{:S(2)}, u32[]{:S(2)}) %collective-permute-start) | collective-permute-done | bytes 4194336 | tf_op jit(solution)/shard_map/ppermute | solution.py:10
  30.2 8.0 %add_select_fusion.1 = f32[8,131072]{1,0:T(8,128)} fusion(f32[8,131072]{1,0:T(8,128)} %collective-permute-done, pred[]{:T(512)S(6)} %eq.7, f32[1,8,1024,128]{3,2,1,0:T(8,128)} %copy-done), kind=kLoop, calls=%fused_computation.8 | loop fusion | flops 3145728 | bytes 12582913 | tf_op jit(solution)/shard_map/jit(_where)/select_n | solution.py:55
  38.1 0.3 collective-permute-start.1
  38.4 91.8 %collective-permute-done.1 = f32[8,131072]{1,0:T(8,128)} collective-permute-done((f32[8,131072]{1,0:T(8,128)}, f32[8,131072]{1,0:T(8,128)}, u32[]{:S(2)}, u32[]{:S(2)}) %collective-permute-start.1) | collective-permute-done | bytes 4194336 | tf_op jit(solution)/shard_map/ppermute | solution.py:10
  130.2 3.9 %add_select_fusion = f32[8,131072]{1,0:T(8,128)S(1)} fusion(f32[8,131072]{1,0:T(8,128)} %add_select_fusion.1, f32[8,131072]{1,0:T(8,128)} %collective-permute-done.1, pred[]{:T(512)S(6)} %eq.6), kind=kLoop, calls=%fused_computation.7 | loop fusion | flops 3145728 | bytes 12582913 | tf_op jit(solution)/shard_map/jit(_where)/select_n | solution.py:55
  134.1 97.0 %all_to_all.10 = f32[8,8,16384]{2,0,1:T(8,128)S(1)} all-to-all(f32[8,8,16384]{2,0,1:T(8,128)S(1)} %bitcast.35), channel_id=1, replica_groups=mesh['wide'=8,'narrow'=4] {'wide'}, dimensions={1} | all-to-all | bytes 8388608 | tf_op jit(solution)/shard_map/all_to_all | solution.py:60
  231.2 5.8 %convolution_bitcast_fusion = f32[8,8,16384]{2,1,0:T(8,128)S(1)} fusion(f32[8,8,16384]{2,0,1:T(8,128)S(1)} %all_to_all.10), kind=kOutput, calls=%fused_computation | convolution fusion | flops 100664128 | bytes 8388608 | tf_op jit(solution)/shard_map/cwr,vw->cvr/dot_general | solution.py:58
  237.0 2.4 copy.8
  239.4 95.9 %all_to_all.11 = f32[8,8,16384]{2,0,1:T(8,128)S(1)} all-to-all(f32[8,8,16384]{2,0,1:T(8,128)S(1)} %copy.8), channel_id=1, replica_groups=mesh['wide'=8,'narrow'=4] {'wide'}, dimensions={1} | all-to-all | bytes 8388608 | tf_op jit(solution)/shard_map/all_to_all | solution.py:64
  335.3 2.4 broadcast_multiply_fusion
Async XLA Ops:
  17.9 4.5 %copy-start = (f32[1,8,1024,128]{3,2,1,0:T(8,128)}, f32[1,8,1024,128]{3,2,1,0:T(8,128)S(1)}, u32[]{:S(2)}) copy-start(f32[1,8,1024,128]{3,2,1,0:T(8,128)S(1)} %convolution_bitcast_fusion.1) | copy-start | bytes 12582916
  22.3 7.8 %collective-permute-start = (f32[8,131072]{1,0:T(8,128)}, f32[8,131072]{1,0:T(8,128)}, u32[]{:S(2)}, u32[]{:S(2)}) collective-permute-start(f32[8,131072]{1,0:T(8,128)} %bitcast.34), channel_id=1, source_target_pairs={{0,1},{1,0},{2,3},{3,2},{4,5},{5,4},{6,7},{7,6},{8,9},{9,8},{10,11... | collective-permute-start | bytes 12582920 | tf_op jit(solution)/shard_map/ppermute | solution.py:10
  38.1 92.1 %collective-permute-start.1 = (f32[8,131072]{1,0:T(8,128)}, f32[8,131072]{1,0:T(8,128)}, u32[]{:S(2)}, u32[]{:S(2)}) collective-permute-start(f32[8,131072]{1,0:T(8,128)} %add_select_fusion.1), channel_id=1, source_target_pairs={{0,2},{1,3},{2,0},{3,1},{4,6},{5,7},{6,4},{7,5},{8,10},{9,11},{10,... | collective-permute-start | bytes 12582920 | tf_op jit(solution)/shard_map/ppermute | solution.py:10
where the time goes:
time: 342 us; the launch traced here: 338 us
  blocking collectives  193 us (56%)
  waiting for transfers between devices  99 us (29%)
  matrix products  19.8 us (6%)
  other arithmetic  18.1 us (5%)
  local copies, waits for them, and re-layouts  6.88 us (2%)
    ppermute x2, waiting for transfers between devices, swapped(): lax.ppermute(shard, axis, [(i, i ^ 1 << distance) for i in range(lax.axis...  99 us
    all_to_all x1, blocking collectives, body(): lax.all_to_all(blocks, 'wide', split_axis=1, concat_axis=1, tiled=True)  97 us
    all_to_all x1, blocking collectives, body(): lax.all_to_all(mixed, 'wide', split_axis=1, concat_axis=1, tiled=True)  95.9 us
    select_n x2, other arithmetic, body(): current = jnp.where(upper_half, partner - current, current + partner)  11.9 us
    dot_general x2, matrix products, local_transform(): jnp.einsum('cafb,gf->cagb', shaped, table, precision=lax.Precision.HIGHEST)  10.4 us
  transfers between devices with their start and end apart: 2, of which 2 were waited for; matrix products, arithmetic and copies ran while one was open for 0% of the time, Pallas kernels for 0%

commit v1 on v0

v1 whole, which is shorter than its diff:
```python
import functools
import math

import jax
import jax.numpy as jnp
from jax import lax
from jax.experimental import pallas as pl
from jax.experimental.pallas import tpu as pltpu
from jax.sharding import PartitionSpec as P

LANES = 128
CHUNKS = 2
RADIX = 32
MESH = pl.DeviceIdType.MESH


def xor(first, second, count):
    total = 0
    for level in range(count.bit_length() - 1):
        one = lax.rem(lax.div(first, 1 << level), 2)
        two = lax.rem(lax.div(second, 1 << level), 2)
        total = total + (one + two - 2 * one * two) * (1 << level)
    return total


def butterflies(values):
    values = list(values)
    half = 1
    while half < len(values):
        for low in range(len(values)):
            if not low & half:
                a, b = values[low], values[low | half]
                values[low], values[low | half] = a + b, a - b
        half *= 2
    return values


def lane_table():
    rows = lax.broadcasted_iota(jnp.int32, (LANES, LANES), 0)
    cols = lax.broadcasted_iota(jnp.int32, (LANES, LANES), 1)
    parity = rows & cols
    for shift in (4, 2, 1):
        parity = parity ^ (parity >> shift)
    return (1 - 2 * (parity & 1)).astype(jnp.float32).astype(jnp.bfloat16)


def mix_slots(load, store, count, scale=None):
    if count <= RADIX:
        values = butterflies([load(i) for i in range(count)])
        for i, value in enumerate(values):
            store(i, value if scale is None else value * scale)
        return
    high = count // RADIX
    held = []
    for group in range(high):
        held.append(butterflies([load(group * RADIX + i) for i in range(RADIX)]))
    for i in range(RADIX):
        values = butterflies([held[group][i] for group in range(high)])
        for group, value in enumerate(values):
            store(group * RADIX + i, value if scale is None else value * scale)


def kernel(wide, narrow, chunks, scale, x_ref, s_ref, o_ref,
           ahead, landed, mixed, back, table,
           ahead_sem, landed_sem, mixed_sem, back_sem):
    count = wide * narrow
    block = x_ref.shape[1] // count
    part = block // chunks
    tiles = part // LANES
    me = lax.axis_index("wide") * narrow + lax.axis_index("narrow")

    def device(index):
        return (lax.div(index, narrow), lax.rem(index, narrow))

    def peer(step):
        half = count // 2
        flip = lax.div(step, 2)
        even = 1 - lax.rem(step, 2)
        return xor(me, flip + even * half + (1 - even), count)

    barrier = pltpu.get_barrier_semaphore()

    def greet(step, carry):
        pl.semaphore_signal(barrier, inc=1, device_id=device(peer(step)), device_id_type=MESH)
        return carry

    lax.fori_loop(0, count - 1, greet, 0)

    table[...] = lane_table()

    def low_bits(index):
        first = pl.multiple_of(index * block, block)
        first_tile = index * (block // LANES)
        values = []
        for t in range(block // LANES):
            sign = (2 * s_ref[pl.ds(first_tile + t, 1), :] - 1).astype(jnp.float32)
            values.append(x_ref[:, pl.ds(pl.multiple_of(first + t * LANES, LANES), LANES)] * sign)
        flat = jnp.concatenate(butterflies(values), axis=0)
        upper = flat.astype(jnp.bfloat16)
        lower = (flat - upper.astype(jnp.float32)).astype(jnp.bfloat16)
        out = jnp.dot(upper, table[...], preferred_element_type=jnp.float32)
        return out + jnp.dot(lower, table[...], preferred_element_type=jnp.float32)

    def keep(ref, index, value):
        for t in range(block // LANES):
            lane = (t % tiles) * LANES
            ref[t // tiles, index, :, lane:lane + LANES] = value[t * 8:(t + 1) * 8, :]

    keep(landed, me, low_bits(me))
    pl.semaphore_wait(barrier, count - 1)

    for chunk in range(chunks):
        def send_ahead(step, carry, chunk=chunk):
            to = peer(step)
            if chunk == 0:
                keep(ahead, to, low_bits(to))
            pltpu.make_async_remote_copy(
                src_ref=ahead.at[chunk, to],
                dst_ref=landed.at[chunk, me],
                send_sem=ahead_sem.at[chunk],
                recv_sem=landed_sem.at[chunk],
                device_id=device(to),
                device_id_type=MESH,
            ).start()
            return carry

        lax.fori_loop(0, count - 1, send_ahead, 0)

    def wait_bytes(ref, chunk, sem):
        spot = ref.at[chunk, pl.ds(0, count - 1)]
        pltpu.make_async_copy(spot, spot, sem.at[chunk]).wait()

    for chunk in range(chunks):
        wait_bytes(landed, chunk, landed_sem)

        def mix(t, carry, chunk=chunk):
            lanes = pl.ds(pl.multiple_of(t * LANES, LANES), LANES)

            def store(i, value):
                mixed[chunk, i, :, lanes] = value

            mix_slots(lambda i: landed[chunk, i, :, lanes], store, count)
            return carry

        lax.fori_loop(0, tiles, mix, 0)

        def send_back(step, carry, chunk=chunk):
            to = peer(step)
            pltpu.make_async_remote_copy(
                src_ref=mixed.at[chunk, to],
                dst_ref=back.at[chunk, me],
                send_sem=mixed_sem.at[chunk],
                recv_sem=back_sem.at[chunk],
                device_id=device(to),
                device_id_type=MESH,
            ).start()
            return carry

        lax.fori_loop(0, count - 1, send_back, 0)
        back[chunk, me] = mixed[chunk, me]

    for chunk in range(chunks):
        wait_bytes(back, chunk, back_sem)

        def finish(t, carry, chunk=chunk):
            lanes = pl.ds(pl.multiple_of(t * LANES, LANES), LANES)

            def store(i, value):
                start = pl.multiple_of(i * block + chunk * part + t * LANES, LANES)
                o_ref[:, pl.ds(start, LANES)] = value

            mix_slots(lambda i: back[chunk, i, :, lanes], store, count, scale)
            return carry

        lax.fori_loop(0, tiles, finish, 0)

    for chunk in range(chunks):
        wait_bytes(ahead, chunk, ahead_sem)
        wait_bytes(mixed, chunk, mixed_sem)


def body(wide, narrow, matrix_panel, sign_bits):
    columns, length = matrix_panel.shape
    count = wide * narrow
    part = length // (count * CHUNKS)
    scale = 1.0 / math.sqrt(length * count)
    slots = pltpu.VMEM((CHUNKS, count, columns, part), jnp.float32)
    return pl.pallas_call(
        functools.partial(kernel, wide, narrow, CHUNKS, scale),
        out_shape=jax.ShapeDtypeStruct((columns, length), jnp.float32),
        in_specs=[pl.BlockSpec(memory_space=pltpu.VMEM)] * 2,
        out_specs=pl.BlockSpec(memory_space=pltpu.VMEM),
        scratch_shapes=[slots] * 4
        + [pltpu.VMEM((LANES, LANES), jnp.bfloat16)]
        + [pltpu.SemaphoreType.DMA((CHUNKS,))] * 4,
        compiler_params=pltpu.CompilerParams(
            collective_id=0, has_side_effects=True, vmem_limit_bytes=48 * 1024 * 1024
        ),
        cost_estimate=pl.CostEstimate(
            flops=4 * columns * length * LANES,
            bytes_accessed=8 * columns * length,
            transcendentals=0,
        ),
    )(matrix_panel, sign_bits.reshape(length // LANES, LANES))


def solution(mesh):
    in_specs = (P(None, ("wide", "narrow")), P(("wide", "narrow")))
    out_specs = P(None, ("wide", "narrow"))
    shape = dict(mesh.shape)
    return jax.shard_map(
        functools.partial(body, shape["wide"], shape["narrow"]),
        mesh=mesh, in_specs=in_specs, out_specs=out_specs, check_vma=False,
    )
```

time: 342 us -> 193 us (0.56); the launches traced: 338 us -> 193 us
  blocking collectives: 193 us -> 0 us
  Pallas kernels: 0 us -> 190 us
  waiting for transfers between devices: 99 us -> 0 us
  matrix products: 19.8 us -> 0 us
  other arithmetic: 18.1 us -> 0 us
  local copies, waits for them, and re-layouts: 6.88 us -> 3.06 us
    all_to_all x2 -> x0, blocking collectives: 193 us -> none  [the longest x1 97 us: body(): lax.all_to_all(blocks, 'wide', split_axis=1, concat_axis=1, tiled=True)]
    pallas_call x0 -> x1, Pallas kernels: none -> 190 us  [body(): pl.pallas_call(functools.partial(kernel, wide, narrow, CHUNKS, scale), ou...]
    ppermute x2 -> x0, waiting for transfers between devices: 99 us -> none  [swapped(): lax.ppermute(shard, axis, [(i, i ^ 1 << distance) for i in range(lax.axis...]
    dot_general x4 -> x0, matrix products: 19.8 us -> none  [the longest x2 10.4 us: local_transform(): jnp.einsum('cafb,gf->cagb', shaped, table, precision=lax.Precision.HIGHEST)]
    select_n x2 -> x0, other arithmetic: 11.9 us -> none  [body(): current = jnp.where(upper_half, partner - current, current + partner)]
    mul x2 -> x0, other arithmetic: 5.08 us -> none  [the longest x1 2.73 us: body(): signed = matrix_panel * (2 * sign_bits - 1).astype(jnp.float32)[None, :]]
  transfers between devices with their start and end apart: 2 -> 0, of which waited for: 2 -> 0; matrix products, arithmetic and copies ran while one was open for 0% -> 0% of each run, Pallas kernels for 0% -> 0%
where the time goes in v1:
time: 193 us
  Pallas kernels  190 us (98%)
  local copies, waits for them, and re-layouts  3.06 us (2%)
    pallas_call x1, Pallas kernels, body(): pl.pallas_call(functools.partial(kernel, wide, narrow, CHUNKS, scale), ou...  190 us

profile of v1, /device:TPU:11, one launch (start us, length us, event | category | flops | bytes accessed | tf_op | source)
XLA Modules:
  0.0 192.8 jit_solution(17913663444141604824)
XLA Ops:
  0.0 0.0 copy-start
  0.0 1.0 copy-done
  1.0 189.7 %shard_map.28 = f32[8,131072]{1,0:T(8,128)S(1)} custom-call(f32[8,131072]{1,0:T(8,128)} %x_ref.1, s32[1024,128]{1,0:T(8,128)S(1)} %bitcast.1), custom_call_target="tpu_custom_call" | custom-call | flops 536870912 | bytes 8388608 | tf_op jit(solution)/shard_map/pallas_call | solution.py:188
  190.8 2.0 %copy.4 = f32[8,131072]{1,0:T(8,128)} copy(f32[8,131072]{1,0:T(8,128)S(1)} %shard_map.28) | data formatting | bytes 8388608
Async XLA Ops:
  0.0 1.0 copy-start

commit v2 on v1

--- a/solution.py
+++ b/solution.py
@@ -9,7 +9,7 @@
 from jax.sharding import PartitionSpec as P
 
 LANES = 128
-CHUNKS = 2
+CHUNKS = 4
 RADIX = 32
 MESH = pl.DeviceIdType.MESH
 
@@ -60,9 +60,9 @@
             store(group * RADIX + i, value if scale is None else value * scale)
 
 
-def kernel(wide, narrow, chunks, scale, x_ref, s_ref, o_ref,
-           ahead, landed, mixed, back, table,
-           ahead_sem, landed_sem, mixed_sem, back_sem):
+def kernel(wide, narrow, chunks, scale, x_hbm, s_hbm, o_ref,
+           x_ref, s_ref, ahead, landed, mixed, back, table,
+           x_sem, s_sem, ahead_sem, landed_sem, mixed_sem, back_sem):
     count = wide * narrow
     block = x_ref.shape[1] // count
     part = block // chunks
@@ -78,6 +78,20 @@
         even = 1 - lax.rem(step, 2)
         return xor(me, flip + even * half + (1 - even), count)
 
+    def fetch(index):
+        spot = (slice(None), pl.ds(pl.multiple_of(index * block, block), block))
+        return pltpu.make_async_copy(x_hbm.at[spot], x_ref.at[spot], x_sem.at[index])
+
+    signs = pltpu.make_async_copy(s_hbm, s_ref, s_sem)
+    signs.start()
+
+    def fetch_peer(step, carry):
+        fetch(peer(step)).start()
+        return carry
+
+    lax.fori_loop(0, count - 1, fetch_peer, 0)
+    fetch(me).start()
+
     barrier = pltpu.get_barrier_semaphore()
 
     def greet(step, carry):
@@ -89,6 +103,7 @@
     table[...] = lane_table()
 
     def low_bits(index):
+        fetch(index).wait()
         first = pl.multiple_of(index * block, block)
         first_tile = index * (block // LANES)
         values = []
@@ -106,25 +121,38 @@
             lane = (t % tiles) * LANES
             ref[t // tiles, index, :, lane:lane + LANES] = value[t * 8:(t + 1) * 8, :]
 
+    signs.wait()
+    keep(ahead, peer(0), low_bits(peer(0)))
+    pl.semaphore_wait(barrier, count - 1)
+
+    def send_ahead(chunk, step):
+        to = peer(step)
+        pltpu.make_async_remote_copy(
+            src_ref=ahead.at[chunk, to],
+            dst_ref=landed.at[chunk, me],
+            send_sem=ahead_sem.at[chunk],
+            recv_sem=landed_sem.at[chunk],
+            device_id=device(to),
+            device_id_type=MESH,
+        ).start()
+
+    def send_then_work(step, carry):
+        send_ahead(0, step)
+        later = peer(step + 1)
+        keep(ahead, later, low_bits(later))
+        return carry
+
+    lax.fori_loop(0, count - 2, send_then_work, 0)
+    send_ahead(0, count - 2)
+
+    for chunk in range(1, chunks):
+        def send(step, carry, chunk=chunk):
+            send_ahead(chunk, step)
+            return carry
+
+        lax.fori_loop(0, count - 1, send, 0)
+
     keep(landed, me, low_bits(me))
-    pl.semaphore_wait(barrier, count - 1)
-
-    for chunk in range(chunks):
-        def send_ahead(step, carry, chunk=chunk):
-            to = peer(step)
-            if chunk == 0:
-                keep(ahead, to, low_bits(to))
-            pltpu.make_async_remote_copy(
-                src_ref=ahead.at[chunk, to],
-                dst_ref=landed.at[chunk, me],
-                send_sem=ahead_sem.at[chunk],
-                recv_sem=landed_sem.at[chunk],
-                device_id=device(to),
-                device_id_type=MESH,
-            ).start()
-            return carry
-
-        lax.fori_loop(0, count - 1, send_ahead, 0)
 
     def wait_bytes(ref, chunk, sem):
         spot = ref.at[chunk, pl.ds(0, count - 1)]
@@ -188,10 +216,15 @@
     return pl.pallas_call(
         functools.partial(kernel, wide, narrow, CHUNKS, scale),
         out_shape=jax.ShapeDtypeStruct((columns, length), jnp.float32),
-        in_specs=[pl.BlockSpec(memory_space=pltpu.VMEM)] * 2,
+        in_specs=[pl.BlockSpec(memory_space=pltpu.HBM)] * 2,
         out_specs=pl.BlockSpec(memory_space=pltpu.VMEM),
-        scratch_shapes=[slots] * 4
+        scratch_shapes=[
+            pltpu.VMEM((columns, length), jnp.float32),
+            pltpu.VMEM((length // LANES, LANES), jnp.int32),
+        ]
+        + [slots] * 4
         + [pltpu.VMEM((LANES, LANES), jnp.bfloat16)]
+        + [pltpu.SemaphoreType.DMA((count,)), pltpu.SemaphoreType.DMA(())]
         + [pltpu.SemaphoreType.DMA((CHUNKS,))] * 4,
         compiler_params=pltpu.CompilerParams(
             collective_id=0, has_side_effects=True, vmem_limit_bytes=48 * 1024 * 1024

time: 193 us -> 194 us (level)
  no operation moved by 1% of the time
where the time goes in v2:
time: 194 us; the launch traced here: 193 us
  Pallas kernels  190 us (98%)
  local copies, waits for them, and re-layouts  3.06 us (2%)
    pallas_call x1, Pallas kernels, body(): pl.pallas_call(functools.partial(kernel, wide, narrow, CHUNKS, scale), ou...  190 us

profile of v2, /device:TPU:11, one launch (start us, length us, event | category | flops | bytes accessed | tf_op | source)
XLA Modules:
  0.0 193.4 jit_solution(9750549124012760801)
XLA Ops:
  0.0 0.0 copy-start
  0.0 1.0 copy-done
  1.0 190.3 %shard_map.28 = f32[8,131072]{1,0:T(8,128)S(1)} custom-call(f32[8,131072]{1,0:T(8,128)} %x_hbm.1, s32[1024,128]{1,0:T(8,128)S(1)} %bitcast.1), custom_call_target="tpu_custom_call" | custom-call | flops 536870912 | bytes 8388608 | tf_op jit(solution)/shard_map/pallas_call | solution.py:216
  191.4 2.0 %copy.4 = f32[8,131072]{1,0:T(8,128)} copy(f32[8,131072]{1,0:T(8,128)S(1)} %shard_map.28) | data formatting | bytes 8388608
Async XLA Ops:
  0.0 1.0 copy-start

commit v3 on v2

--- a/solution.py
+++ b/solution.py
@@ -78,36 +78,47 @@
         even = 1 - lax.rem(step, 2)
         return xor(me, flip + even * half + (1 - even), count)
 
+    rows = block // LANES
+
     def fetch(index):
         spot = (slice(None), pl.ds(pl.multiple_of(index * block, block), block))
-        return pltpu.make_async_copy(x_hbm.at[spot], x_ref.at[spot], x_sem.at[index])
-
-    signs = pltpu.make_async_copy(s_hbm, s_ref, s_sem)
-    signs.start()
+        signs = (pl.ds(pl.multiple_of(index * rows, rows), rows),)
+        return (
+            pltpu.make_async_copy(x_hbm.at[spot], x_ref.at[spot], x_sem.at[index]),
+            pltpu.make_async_copy(s_hbm.at[signs], s_ref.at[signs], s_sem.at[index]),
+        )
+
+    def start_fetch(index):
+        for copy in fetch(index):
+            copy.start()
+
+    barrier = pltpu.get_barrier_semaphore()
+
+    def greet(step, carry):
+        other = lax.rem(me + 1 + step, count)
+        pl.semaphore_signal(barrier, inc=1, device_id=device(other), device_id_type=MESH)
+        return carry
+
+    start_fetch(peer(0))
+    start_fetch(peer(1))
+    lax.fori_loop(0, count - 1, greet, 0)
 
     def fetch_peer(step, carry):
-        fetch(peer(step)).start()
+        start_fetch(peer(step))
         return carry
 
-    lax.fori_loop(0, count - 1, fetch_peer, 0)
-    fetch(me).start()
-
-    barrier = pltpu.get_barrier_semaphore()
-
-    def greet(step, carry):
-        pl.semaphore_signal(barrier, inc=1, device_id=device(peer(step)), device_id_type=MESH)
-        return carry
-
-    lax.fori_loop(0, count - 1, greet, 0)
+    lax.fori_loop(2, count - 1, fetch_peer, 0)
+    start_fetch(me)
 
     table[...] = lane_table()
 
     def low_bits(index):
-        fetch(index).wait()
+        for copy in fetch(index):
+            copy.wait()
         first = pl.multiple_of(index * block, block)
-        first_tile = index * (block // LANES)
+        first_tile = index * rows
         values = []
-        for t in range(block // LANES):
+        for t in range(rows):
             sign = (2 * s_ref[pl.ds(first_tile + t, 1), :] - 1).astype(jnp.float32)
             values.append(x_ref[:, pl.ds(pl.multiple_of(first + t * LANES, LANES), LANES)] * sign)
         flat = jnp.concatenate(butterflies(values), axis=0)
@@ -117,11 +128,10 @@
         return out + jnp.dot(lower, table[...], preferred_element_type=jnp.float32)
 
     def keep(ref, index, value):
-        for t in range(block // LANES):
+        for t in range(rows):
             lane = (t % tiles) * LANES
             ref[t // tiles, index, :, lane:lane + LANES] = value[t * 8:(t + 1) * 8, :]
 
-    signs.wait()
     keep(ahead, peer(0), low_bits(peer(0)))
     pl.semaphore_wait(barrier, count - 1)
 
@@ -224,7 +234,7 @@
         ]
         + [slots] * 4
         + [pltpu.VMEM((LANES, LANES), jnp.bfloat16)]
-        + [pltpu.SemaphoreType.DMA((count,)), pltpu.SemaphoreType.DMA(())]
+        + [pltpu.SemaphoreType.DMA((count,))] * 2
         + [pltpu.SemaphoreType.DMA((CHUNKS,))] * 4,
         compiler_params=pltpu.CompilerParams(
             collective_id=0, has_side_effects=True, vmem_limit_bytes=48 * 1024 * 1024
@@ -234,7 +244,10 @@
             bytes_accessed=8 * columns * length,
             transcendentals=0,
         ),
-    )(matrix_panel, sign_bits.reshape(length // LANES, LANES))
+    )(
+        matrix_panel,
+        pltpu.with_memory_space_constraint(sign_bits.reshape(length // LANES, LANES), pltpu.HBM),
+    )
 
 
 def solution(mesh):

time: 194 us -> 190 us (0.979)
  Pallas kernels: 190 us -> 188 us
    pallas_call x1, Pallas kernels: 190 us -> 188 us  [body(): pl.pallas_call(functools.partial(kernel, wide, narrow, CHUNKS, scale), ou...]
where the time goes in v3:
time: 190 us
  Pallas kernels  188 us (99%)
  local copies, waits for them, and re-layouts  2.02 us (1%)
    pallas_call x1, Pallas kernels, body(): pl.pallas_call(functools.partial(kernel, wide, narrow, CHUNKS, scale), ou...  188 us

profile of v3, /device:TPU:11, one launch (start us, length us, event | category | flops | bytes accessed | tf_op | source)
XLA Modules:
  0.0 189.9 jit_solution(10047756919320485929)
XLA Ops:
  0.0 187.9 %shard_map.28 = f32[8,131072]{1,0:T(8,128)S(1)} custom-call(f32[8,131072]{1,0:T(8,128)} %x_hbm.1, s32[1024,128]{1,0:T(8,128)} %bitcast.1), custom_call_target="tpu_custom_call" | custom-call | flops 536870912 | bytes 8388608 | tf_op jit(solution)/shard_map/pallas_call | solution.py:226
  187.9 2.0 %copy.4 = f32[8,131072]{1,0:T(8,128)} copy(f32[8,131072]{1,0:T(8,128)S(1)} %shard_map.28) | data formatting | bytes 8388608

commit v4 on v3

--- a/solution.py
+++ b/solution.py
@@ -9,7 +9,7 @@
 from jax.sharding import PartitionSpec as P
 
 LANES = 128
-CHUNKS = 4
+CHUNKS = 2
 RADIX = 32
 MESH = pl.DeviceIdType.MESH
 

time: 190 us -> 190 us (level)
  no operation moved by 1% of the time
where the time goes in v4:
time: 190 us
  Pallas kernels  188 us (99%)
  local copies, waits for them, and re-layouts  2.02 us (1%)
    pallas_call x1, Pallas kernels, body(): pl.pallas_call(functools.partial(kernel, wide, narrow, CHUNKS, scale), ou...  188 us

profile of v4, /device:TPU:11, one launch (start us, length us, event | category | flops | bytes accessed | tf_op | source)
XLA Modules:
  0.0 189.6 jit_solution(3195344679019872056)
XLA Ops:
  0.0 187.6 %shard_map.28 = f32[8,131072]{1,0:T(8,128)S(1)} custom-call(f32[8,131072]{1,0:T(8,128)} %x_hbm.1, s32[1024,128]{1,0:T(8,128)} %bitcast.1), custom_call_target="tpu_custom_call" | custom-call | flops 536870912 | bytes 8388608 | tf_op jit(solution)/shard_map/pallas_call | solution.py:226
  187.6 2.0 %copy.4 = f32[8,131072]{1,0:T(8,128)} copy(f32[8,131072]{1,0:T(8,128)S(1)} %shard_map.28) | data formatting | bytes 8388608

commit v5 on v3

--- a/solution.py
+++ b/solution.py
@@ -94,14 +94,18 @@
 
     barrier = pltpu.get_barrier_semaphore()
 
-    def greet(step, carry):
-        other = lax.rem(me + 1 + step, count)
-        pl.semaphore_signal(barrier, inc=1, device_id=device(other), device_id_type=MESH)
-        return carry
+    here = (lax.axis_index("wide"), lax.axis_index("narrow"))
+    across = [lax.rem(here[0] + i, wide) for i in range(wide)]
+    along = [lax.rem(here[1] + i, narrow) for i in range(narrow)]
+    for i in sorted(range(wide), key=lambda i: abs(2 * i - wide)):
+        for j in range(narrow):
+            if i or j:
+                pl.semaphore_signal(
+                    barrier, inc=1, device_id=(across[i], along[j]), device_id_type=MESH
+                )
 
     start_fetch(peer(0))
     start_fetch(peer(1))
-    lax.fori_loop(0, count - 1, greet, 0)
 
     def fetch_peer(step, carry):
         start_fetch(peer(step))

time: 190 us -> 190 us (level)
  no operation moved by 1% of the time
where the time goes in v5:
time: 190 us
  Pallas kernels  188 us (99%)
  local copies, waits for them, and re-layouts  2.02 us (1%)
    pallas_call x1, Pallas kernels, body(): pl.pallas_call(functools.partial(kernel, wide, narrow, CHUNKS, scale), ou...  188 us

profile of v5, /device:TPU:11, one launch (start us, length us, event | category | flops | bytes accessed | tf_op | source)
XLA Modules:
  0.0 190.3 jit_solution(1020903281076275619)
XLA Ops:
  0.0 188.3 %shard_map.28 = f32[8,131072]{1,0:T(8,128)S(1)} custom-call(f32[8,131072]{1,0:T(8,128)} %x_hbm.1, s32[1024,128]{1,0:T(8,128)} %bitcast.1), custom_call_target="tpu_custom_call" | custom-call | flops 536870912 | bytes 8388608 | tf_op jit(solution)/shard_map/pallas_call | solution.py:230
  188.3 2.0 %copy.4 = f32[8,131072]{1,0:T(8,128)} copy(f32[8,131072]{1,0:T(8,128)S(1)} %shard_map.28) | data formatting | bytes 8388608

commit v6 on v5

--- a/solution.py
+++ b/solution.py
@@ -9,7 +9,7 @@
 from jax.sharding import PartitionSpec as P
 
 LANES = 128
-CHUNKS = 4
+CHUNKS = 2
 RADIX = 32
 MESH = pl.DeviceIdType.MESH
 
@@ -76,7 +76,7 @@
         half = count // 2
         flip = lax.div(step, 2)
         even = 1 - lax.rem(step, 2)
-        return xor(me, flip + even * half + (1 - even), count)
+        return xor(me, even * (count - 1 - flip) + (1 - even) * (half - 1 - flip), count)
 
     rows = block // LANES
 

time: 190 us -> 195 us (1.026)
  the two profiles are of different devices: /device:TPU:11 before, /device:TPU:0 now
where the time goes in v6:
time: 195 us
  Pallas kernels  193 us (99%)
  local copies, waits for them, and re-layouts  2.02 us (1%)
    pallas_call x1, Pallas kernels, body(): pl.pallas_call(functools.partial(kernel, wide, narrow, CHUNKS, scale), ou...  193 us

profile of v6, /device:TPU:0, one launch (start us, length us, event | category | flops | bytes accessed | tf_op | source)
XLA Modules:
  0.0 194.5 jit_solution(12783531961839082294)
XLA Ops:
  0.0 192.5 %shard_map.28 = f32[8,131072]{1,0:T(8,128)S(1)} custom-call(f32[8,131072]{1,0:T(8,128)} %x_hbm.1, s32[1024,128]{1,0:T(8,128)} %bitcast.1), custom_call_target="tpu_custom_call" | custom-call | flops 536870912 | bytes 8388608 | tf_op jit(solution)/shard_map/pallas_call | solution.py:230
  192.5 2.0 %copy.4 = f32[8,131072]{1,0:T(8,128)} copy(f32[8,131072]{1,0:T(8,128)S(1)} %shard_map.28) | data formatting | bytes 8388608

commit v7 on v6

--- a/solution.py
+++ b/solution.py
@@ -73,10 +73,11 @@
         return (lax.div(index, narrow), lax.rem(index, narrow))
 
     def peer(step):
-        half = count // 2
-        flip = lax.div(step, 2)
+        half, quarter = count // 2, count // 4
         even = 1 - lax.rem(step, 2)
-        return xor(me, even * (count - 1 - flip) + (1 - even) * (half - 1 - flip), count)
+        place = lax.div(step, 2) + 1 - even
+        turn = lax.rem(place, 2) * quarter + lax.div(place, 2)
+        return xor(me, turn + even * half, count)
 
     rows = block // LANES
 

time: 195 us -> 191 us (0.979)
  the two profiles are of different devices: /device:TPU:0 before, /device:TPU:11 now
where the time goes in v7:
time: 191 us
  Pallas kernels  189 us (99%)
  local copies, waits for them, and re-layouts  2.02 us (1%)
    pallas_call x1, Pallas kernels, body(): pl.pallas_call(functools.partial(kernel, wide, narrow, CHUNKS, scale), ou...  189 us

profile of v7, /device:TPU:11, one launch (start us, length us, event | category | flops | bytes accessed | tf_op | source)
XLA Modules:
  0.0 190.7 jit_solution(11467147831013341362)
XLA Ops:
  0.0 188.7 %shard_map.28 = f32[8,131072]{1,0:T(8,128)S(1)} custom-call(f32[8,131072]{1,0:T(8,128)} %x_hbm.1, s32[1024,128]{1,0:T(8,128)} %bitcast.1), custom_call_target="tpu_custom_call" | custom-call | flops 536870912 | bytes 8388608 | tf_op jit(solution)/shard_map/pallas_call | solution.py:231
  188.7 2.0 %copy.4 = f32[8,131072]{1,0:T(8,128)} copy(f32[8,131072]{1,0:T(8,128)S(1)} %shard_map.28) | data formatting | bytes 8388608

commit v8 on v6

--- a/solution.py
+++ b/solution.py
@@ -73,10 +73,9 @@
         return (lax.div(index, narrow), lax.rem(index, narrow))
 
     def peer(step):
+        step = jnp.int32(step)
         half = count // 2
-        flip = lax.div(step, 2)
-        even = 1 - lax.rem(step, 2)
-        return xor(me, even * (count - 1 - flip) + (1 - even) * (half - 1 - flip), count)
+        return xor(me, lax.select(step < half, half + step, step - half + 1), count)
 
     rows = block // LANES
 

time: 195 us -> 197 us (1.010)
  the two profiles are of different devices: /device:TPU:0 before, /device:TPU:11 now
where the time goes in v8:
time: 197 us; the launch traced here: 195 us
  Pallas kernels  193 us (98%)
  local copies, waits for them, and re-layouts  2.02 us (1%)
    pallas_call x1, Pallas kernels, body(): pl.pallas_call(functools.partial(kernel, wide, narrow, CHUNKS, scale), ou...  193 us

profile of v8, /device:TPU:11, one launch (start us, length us, event | category | flops | bytes accessed | tf_op | source)
XLA Modules:
  0.0 195.5 jit_solution(6626346086625237044)
XLA Ops:
  0.0 193.5 %shard_map.28 = f32[8,131072]{1,0:T(8,128)S(1)} custom-call(f32[8,131072]{1,0:T(8,128)} %x_hbm.1, s32[1024,128]{1,0:T(8,128)} %bitcast.1), custom_call_target="tpu_custom_call" | custom-call | flops 536870912 | bytes 8388608 | tf_op jit(solution)/shard_map/pallas_call | solution.py:229
  193.5 2.0 %copy.4 = f32[8,131072]{1,0:T(8,128)} copy(f32[8,131072]{1,0:T(8,128)S(1)} %shard_map.28) | data formatting | bytes 8388608
